TPU v7x, 512 devices: a whole 4x4x16 slice. The times are simulated.
512 devices in a mesh: span: 8 (over z_hi, core), seq: 16 (over z_lo, y), tensor: 4 (over x).
Axes of the slice: x: 4, y: 4, z: 16 (z_hi: 4, z_lo: 4; z = z_hi * 4 + z_lo), core: 2. Of those that a mesh axis runs over, the one named last changes fastest.
Arguments:
- queries: bfloat16 [8192, 3072], P(('span', 'seq'), 'tensor'), may hold values from -20 to 20
- key_value_pairs: bfloat16 [8192, 2, 512], P(('span', 'seq'), None, 'tensor'), may hold values from -20 to 20
- out_weight: bfloat16 [3072, 3072], P('tensor', 'seq'), may hold values from -0.109375 to 0.109375
- gate_table: float32 [64, 3072], P(None, 'tensor'), may hold values from -4 to 4
- norm_gain: float32 [3072], P('tensor'), may hold values from 0.5 to 1.5
- plan: int32 [8], replicated, may hold values from 0 to 7, each once
- noise_level: int32 [8], replicated, may hold values from 0 to 63
- span_mask: int32 [8, 8, 16], replicated, may hold values from 0 to 1, as said below
Outputs:
- attended: bfloat16 [8192, 3072], P(('span', 'seq'), 'tensor')
Inputs may be any that keep to these rules, and one draw needn't show every extreme that they name: `span_mask`: entry [p, q, f] is 1 where q == p and 0 where q > p.
All inputs are finite; a program needn't handle non-finite values.
Results may differ from a plain program's by a relative error of at most 0.018.
Values may be sent and summed in bfloat16 or wider, within the bound.
A program may use at most 64 MiB of HBM per device.

v0:
```python
import math

import jax
import jax.numpy as jnp
from jax import lax
from jax.sharding import PartitionSpec as P

HEAD_WIDTH = 128


def local(
    queries, key_value_pairs, out_weight, gate_table, norm_gain, plan, noise_level, span_mask
):
    rows = queries.shape[0]
    kv_heads = key_value_pairs.shape[2] // HEAD_WIDTH
    q_heads = queries.shape[1] // HEAD_WIDTH
    heads_per_group = q_heads // kv_heads
    scale = 1.0 / math.sqrt(HEAD_WIDTH)
    n_span = lax.axis_size("span")
    frame_count = span_mask.shape[2]
    span_rows = rows * lax.axis_size("seq")
    frame_rows = span_rows // frame_count
    groups = jnp.arange(n_span, dtype=jnp.int32)
    mine_group = lax.axis_index("span")
    position = jnp.sum(jnp.where(groups == mine_group, plan, 0))
    mask_row = jnp.sum(jnp.where((groups == position)[:, None, None], span_mask, 0), axis=0)
    visible_group = jnp.sum(
        jnp.where((plan[:, None] == groups[None, :])[:, :, None], mask_row[None, :, :], 0), axis=1
    )
    visible_flat = visible_group.reshape(n_span * frame_count)
    slot_ids = jnp.arange(n_span * frame_count, dtype=jnp.int32)
    level_now = jnp.sum(jnp.where(groups == mine_group, noise_level, 0))
    query_heads = queries.reshape(rows, kv_heads, heads_per_group, HEAD_WIDTH)

    def update(state, key_block, seen):
        best, total, accum = state
        key_rows = key_block[:, 0]
        value_rows = key_block[:, 1]
        scores = (
            jnp.einsum("tkgd,rkd->tkgr", query_heads, key_rows, preferred_element_type=jnp.float32)
            * scale
        )
        scores = jnp.where(seen, scores, -1e30)
        peak = jnp.maximum(best, jnp.max(scores, axis=-1))
        weights = jnp.where(seen, jnp.exp(scores - peak[..., None]), 0.0)
        fade = jnp.exp(best - peak)
        total = total * fade + jnp.sum(weights, axis=-1)
        added = jnp.einsum(
            "tkgr,rkd->tkgd",
            weights.astype(jnp.bfloat16),
            value_rows,
            preferred_element_type=jnp.float32,
        )
        return (peak, total, accum * fade[..., None] + added)

    initial = (
        jnp.full((rows, kv_heads, heads_per_group), -1e30, jnp.float32),
        jnp.zeros((rows, kv_heads, heads_per_group), jnp.float32),
        jnp.zeros((rows, kv_heads, heads_per_group, HEAD_WIDTH), jnp.float32),
    )
    carry = initial
    piece = lax.all_gather(key_value_pairs, ("span", "seq"), axis=0, tiled=True)
    width = piece.shape[0]
    token_block = math.gcd(width, 2048)
    blocks = piece.reshape(width // token_block, token_block, 2, kv_heads, HEAD_WIDTH)

    def step(state, item):
        key_block, index = item
        row_ids = index * token_block + jnp.arange(token_block, dtype=jnp.int32)
        owner = row_ids // span_rows
        frame = row_ids % span_rows // frame_rows
        slot = owner * frame_count + frame
        seen = (
            jnp.sum(jnp.where(slot[:, None] == slot_ids[None, :], visible_flat[None, :], 0), axis=1)
            > 0
        )
        return (update(state, key_block, seen), None)

    carry, unused = lax.scan(
        step, carry, (blocks, jnp.arange(width // token_block, dtype=jnp.int32))
    )
    best, total, accum = carry
    heads_out = (accum / total[..., None]).reshape(rows, q_heads * HEAD_WIDTH).astype(jnp.bfloat16)
    partial_sums = jnp.dot(
        heads_out,
        lax.all_gather(out_weight, "seq", axis=1, tiled=True),
        preferred_element_type=jnp.float32,
    )
    columns = gate_table.shape[1]
    summed = lax.psum(partial_sums.astype(jnp.bfloat16), "tensor").astype(jnp.float32)
    power = jnp.mean(summed * summed, axis=-1)
    own_cols = lax.dynamic_slice_in_dim(summed, lax.axis_index("tensor") * columns, columns, 1)
    levels = jnp.arange(gate_table.shape[0], dtype=jnp.int32)
    gate = jnp.sum(jnp.where((levels == level_now)[:, None], gate_table, 0.0), axis=0)
    result = own_cols * lax.rsqrt(power + 1e-06)[:, None] * norm_gain * gate
    return result.astype(jnp.bfloat16)


def solution(mesh):
    return jax.shard_map(
        local,
        mesh=mesh,
        in_specs=(
            P(("span", "seq"), "tensor"),
            P(("span", "seq"), None, "tensor"),
            P("tensor", "seq"),
            P(None, "tensor"),
            P("tensor"),
            P(),
            P(),
            P(),
        ),
        out_specs=P(("span", "seq"), "tensor"),
        check_vma=False,
    )
```

profile of v0, /device:TPU:1, one launch (start us, length us, event | category | flops | bytes accessed | tf_op | source)
XLA Modules:
  0.0 548.7 jit_solution(16727510897713443667)
XLA Ops:
  6.5 1.4 copy.13
  8.0 0.7 all-gather.5.cloned.1.call-update
  8.8 0.7 iota_compare_fusion.1
  9.5 1.3 fusion.32
  10.8 0.6 iota_compare_fusion.3
  11.5 0.8 select_reduce_fusion.3
  12.3 0.1 select_reduce_fusion.2
  12.4 0.1 broadcast_in_dim.170
  12.5 1.0 reshape.161
  13.6 368.3 %all-gather.3.cloned.1.call-done = bf16[8192,2,128]{2,0,1:T(8,128)(2,1)} async-done(((bf16[64,2,128]{2,0,1:T(8,128)(2,1)}), bf16[8192,2,128]{2,0,1:T(8,128)(2,1)}) %all-gather.3.cloned.1.call-update) | async-done | bytes 4194320 | tf_op jit(solution)/shard_map/all_gather | solution.py:62
  381.9 29.6 %while.19 = (s32[]{:T(128)}, f32[64,1,6]{0,2,1:T(8,128)S(1)}, f32[64,1,6]{0,2,1:T(8,128)S(1)}, f32[64,1,6,128]{3,0,2,1:T(8,128)S(1)}, s32[4]{0:T(128)S(1)}, /*in...) while((s32[]{:T(128)}, f32[64,1,6]{0,2,1:T(8,128)S(1)}, ...), condition=%wide.wide.region_7.8_spmd.clone, body=%wide.wide.region_3.0_spmd.clone.sunk | while | flops 410743040 | bytes 17334972 | solution.py:79
  381.9 0.6 dynamic_slice.29
  383.2 0.6 select_reduce_fusion.6
  383.8 1.3 dynamic-slice_bitcast_fusion.3
  385.1 1.0 copy-done
  386.2 0.7 bitcast_reduce_fusion.3
  386.9 1.8 fusion.49
  388.6 0.6 fusion.48
  389.3 0.6 dynamic_slice.29
  390.6 0.6 select_reduce_fusion.6
  391.2 1.3 dynamic-slice_bitcast_fusion.3
  392.5 1.0 copy-done
  393.6 0.7 bitcast_reduce_fusion.3
  394.3 1.8 fusion.49
  396.0 0.6 fusion.48
  396.7 0.6 dynamic_slice.29
  398.0 0.6 select_reduce_fusion.6
  398.6 1.3 dynamic-slice_bitcast_fusion.3
  400.0 1.0 copy-done
  401.0 0.7 bitcast_reduce_fusion.3
  401.7 1.8 fusion.49
  403.4 0.6 fusion.48
  404.1 0.6 dynamic_slice.29
  405.4 0.6 select_reduce_fusion.6
  406.0 1.3 dynamic-slice_bitcast_fusion.3
  407.4 1.0 copy-done
  408.4 0.7 bitcast_reduce_fusion.3
  409.1 1.8 fusion.49
  410.9 0.6 fusion.48
  411.6 0.1 divide_convert_fusion
  411.8 60.5 %all-gather.5.cloned.1.call-done = bf16[768,3072]{0,1:T(8,128)(2,1)} async-done(((bf16[768,192]{0,1:T(8,128)(2,1)}), bf16[768,3072]{0,1:T(8,128)(2,1)}) %all-gather.5.cloned.1.call-update) | async-done | bytes 4718608 | tf_op jit(solution)/shard_map/all_gather | solution.py:86
  472.3 4.6 convolution_convert_fusion
  477.0 0.6 iota_compare_fusion.2
  477.6 0.1 select_reduce_fusion.1
  477.7 61.5 %all-reduce.2.cloned.1.call-done = bf16[64,3072]{1,0:T(8,128)(2,1)} async-done(((bf16[64,3072]{1,0:T(8,128)(2,1)}), bf16[64,3072]{1,0:T(8,128)(2,1)}) %all-reduce.2.cloned.1.call-update) | async-done | bytes 393232 | tf_op jit(solution)/shard_map/psum | solution.py:90
  539.2 1.2 multiply_reduce_fusion
  540.4 1.1 convert_element_type.25
  541.5 0.7 multiply_convert_fusion
  (42 shorter events, 0.5 us)
Async XLA Ops:
  6.5 375.4 %all-gather.3.cloned.1.call-start = ((), (), s32[]{:S(2)}) async-start(), calls=%async_computation | async-start | bytes 4227072 | tf_op jit(solution)/shard_map/all_gather | solution.py:62
  7.9 464.4 %all-gather.5.cloned.1.call-start = ((), (), s32[]{:S(2)}) async-start(), calls=%async_computation.1 | async-start | bytes 5013504 | tf_op jit(solution)/shard_map/all_gather | solution.py:86
  8.7 530.5 %all-reduce.2.cloned.1.call-start = ((), (), s32[]{:S(2)}) async-start(), calls=%async_computation.2 | async-start | bytes 786432 | tf_op jit(solution)/shard_map/psum | solution.py:90
  12.4 369.5 %copy-start.2 = (s32[8,16]{1,0:T(8,128)}, s32[8,16]{1,0:T(8,128)S(1)}, u32[]{:S(2)}) copy-start(s32[8,16]{1,0:T(8,128)S(1)} %select_reduce_fusion.2) | copy-start | bytes 1540
  385.1 1.0 copy-start
  392.5 1.0 copy-start
  399.9 1.0 copy-start
  407.4 1.0 copy-start
  411.5 66.0 %copy-start.1 = (f32[64,768]{1,0:T(8,128)S(1)}, f32[64,768]{1,0:T(8,128)}, u32[]{:S(2)}) copy-start(f32[64,768]{1,0:T(8,128)} %param.13) | copy-start | bytes 589828
  472.3 69.2 %copy-start.3 = (f32[768]{0:T(1024)S(1)}, f32[768]{0:T(1024)}, u32[]{:S(2)}) copy-start(f32[768]{0:T(1024)} %param.14) | copy-start | bytes 9220
Sparse Core Ops, SparseCore 0:
  9.5 372.3 all-gather.2
  384.0 88.2 all-gather.4
  477.1 62.0 all-reduce.1
where the time goes:
time: 551 us; the launch traced here: 549 us
  waiting for transfers between devices  491 us (89%)
  matrix products  14.4 us (3%)
  local copies, waits for them, and re-layouts  14.3 us (3%)
  between operations  13.3 us (2%)
  other arithmetic  12.7 us (2%)
    all_gather x1, waiting for transfers between devices, local(): piece = lax.all_gather(key_value_pairs, ('span', 'seq'), axis=0, tiled=True)  368 us
    psum x1, waiting for transfers between devices, local(): lax.psum(partial_sums.astype(jnp.bfloat16), 'tensor').astype(jnp.float32)  61.5 us
    all_gather x1, waiting for transfers between devices, local(): lax.all_gather(out_weight, 'seq', axis=1, tiled=True)  60.5 us
  transfers between devices with their start and end apart: 3, of which 3 were waited for; matrix products, arithmetic and copies ran while one was open for 5% of the time, Pallas kernels for 0%

commit v1 on v0

v1 whole, which is shorter than its diff:
```python
import functools
import math

import jax
import jax.numpy as jnp
from jax import lax
from jax.experimental import pallas as pl
from jax.experimental.pallas import tpu as pltpu
from jax.sharding import PartitionSpec as P

MESH = pl.DeviceIdType.MESH
F32, BF16 = jnp.float32, jnp.bfloat16
LOG2E = 1.4426950408889634
SCALE = LOG2E / math.sqrt(128)
NEAR = (1, -1, 2, -2)
FAR = (5, -5)
YS = (1, -1, 2)
XS = (2, 1, -1)
SLOTS = (0, 1, -1, 2, -2, 5, 6, 4, 7, 3, -5, -4, -6, -3, -7, 8)
GROUPS = ((0, 5), (5, 10), (10, 16))
NT = (((1,), (1,)), ((), ()))


def kernel(
    q_ref, kv_ref, w_ref, gate_ref, gain_ref, plan_ref, level_ref, mask_ref, out_ref,
    kvb, qs, kc, vc, acc, peak, part_s, part_r, lse_s, lse_r, heads, wb, ps, pr, pw_s, pw_r,
    ss, rs,
):
    span, seq, x = lax.axis_index("span"), lax.axis_index("seq"), lax.axis_index("tensor")
    core, z_hi = span % 2, span // 2
    z_lo, y = seq // 4, seq % 4
    z = z_hi * 4 + z_lo

    def dev(dx=0, dy=0, dz=0, flip=False):
        zz = (z + dz + 16) % 16
        cc = 1 - core if flip else core
        return ((zz // 4) * 2 + cc, (zz % 4) * 4 + (y + dy + 4) % 4, (x + dx + 4) % 4)

    barrier = pltpu.get_barrier_semaphore()
    partners = [dev(dz=d) for d in (1, -1, 2, -2, 3, -3, 5, -5)]
    partners += [dev(dy=d) for d in YS] + [dev(dx=d) for d in XS] + [dev(flip=True)]
    for p in partners:
        pl.semaphore_signal(barrier, inc=1, device_id=p, device_id_type=MESH)

    row = lax.broadcasted_iota(jnp.int32, (128, 128), 0)
    col = lax.broadcasted_iota(jnp.int32, (128, 128), 1)
    pick = jnp.where(col == 2 * (row % 64) + row // 64, 1.0, 0.0).astype(BF16)
    kvb[0, 0] = jnp.dot(pick, kv_ref[...], preferred_element_type=F32).astype(BF16)
    for h in range(6):
        qs[0, h * 64 : (h + 1) * 64, :] = q_ref[:, h * 128 : (h + 1) * 128]
    half = pl.multiple_of(core * 96, 16)
    rows_a = pl.ds(half, 48)
    rows_b = pl.ds(pl.multiple_of(half + 48, 16), 48)
    wb[z_lo, y, pl.ds(half, 96), :] = w_ref[pl.ds(half, 96), :]

    started = []

    def send(src, dst, to):
        i = len(started)
        c = pltpu.make_async_remote_copy(
            src_ref=src, dst_ref=dst, send_sem=ss.at[i], recv_sem=rs.at[i], device_id=to, device_id_type=MESH
        )
        c.start()
        started.append(c)
        return c

    def near(group):
        lo = GROUPS[group][0]
        return [send(kvb.at[0, lo], kvb.at[0, lo + 1 + i], dev(dz=-d)) for i, d in enumerate(NEAR)]

    def across(group):
        lo, hi = GROUPS[group]
        part = pl.ds(lo, hi - lo)
        return send(kvb.at[0, part], kvb.at[1, part], dev(flip=True))

    def arrived(copies):
        for c in copies:
            c.wait_recv()

    pl.semaphore_wait(barrier, len(partners))

    far = [send(kvb.at[0, 0], kvb.at[0, GROUPS[1 + i][0]], dev(dz=-d)) for i, d in enumerate(FAR)]
    near0 = near(0)
    q_in = [send(qs.at[0], qs.at[1 + i], dev(dy=-d)) for i, d in enumerate(YS)]
    w_b1 = [send(wb.at[z_lo, y, rows_b], wb.at[z_lo, y, rows_b], dev(dy=-d)) for d in YS]
    arrived(near0)
    across0 = across(0)
    arrived(far)
    near1, near2 = near(1), near(2)
    far_slot = GROUPS[1][0] + 5 * core
    eighth = send(kvb.at[0, far_slot], kvb.at[0, 15], dev(dz=6 * core - 3))
    far2 = 4 * core - 2
    z_to = (-1, 1, far2)
    w_a1 = [send(wb.at[z_lo, y, rows_a], wb.at[z_lo, y, rows_a], dev(dz=d)) for d in z_to]

    own_place = plan_ref[span]

    def ingest(group):
        lo, hi = GROUPS[group]
        own_k = kvb[0, 0, 0:64, :]
        i = 0
        for rc in (0, 1):
            for slot in range(lo, hi):
                zz = (z + SLOTS[slot] + 16) % 16
                there = (zz // 4) * 2 + (core if rc == 0 else 1 - core)
                seen = mask_ref[own_place, plan_ref[there], (zz % 4) * 4 + y] > 0
                at = slice(i * 64, (i + 1) * 64)
                kc[at, :] = jnp.where(seen, kvb[rc, slot, 0:64, :], own_k)
                vc[at, 0:128] = jnp.where(seen, kvb[rc, slot, 64:128, :], jnp.zeros((64, 128), BF16))
                vc[at, 128:256] = jnp.where(seen, jnp.ones((64, 128), BF16), jnp.zeros((64, 128), BF16))
                i += 1
        return i * 64

    def unit(k, keys, first):
        for r in range(0, 384, 128):
            rr = slice(r, r + 128)
            s = lax.dot_general(qs[k, rr, :], kc[0:keys, :], NT, preferred_element_type=F32)
            cols = [s[:, t : t + 128] for t in range(0, keys, 128)]
            top = functools.reduce(jnp.maximum, cols)
            top = jnp.broadcast_to(jnp.max(top, axis=1, keepdims=True) * SCALE, (128, 128))
            if not first:
                old = peak[k, rr, :]
                top = jnp.maximum(old, top)
            weights = jnp.concatenate([jnp.exp2(t * SCALE - top).astype(BF16) for t in cols], axis=1)
            added = jnp.dot(weights, vc[0:keys, :], preferred_element_type=F32)
            if first:
                acc[k, rr, :] = added
            else:
                fade = jnp.exp2(old - top)
                acc[k, rr, :] = acc[k, rr, :] * jnp.concatenate([fade, fade], axis=1) + added
            peak[k, rr, :] = top

    across0.wait_recv()
    keys = ingest(0)
    unit(0, keys, True)
    arrived(q_in)
    for k in (1, 2, 3):
        unit(k, keys, True)

    arrived(near1)
    across1 = across(1)
    arrived(w_b1)
    w_b2 = [send(wb.at[z_lo, :, rows_b], wb.at[z_lo, :, rows_b], dev(dz=d)) for d in z_to]
    w_sib = [send(wb.at[z_lo, :, rows_b], wb.at[z_lo, :, rows_b], dev(flip=True))]
    across1.wait_recv()
    keys = ingest(1)
    for k in range(4):
        unit(k, keys, False)

    arrived(near2)
    eighth.wait_recv()
    across2 = across(2)
    arrived(w_a1)
    w_a2 = [send(wb.at[:, y, rows_a], wb.at[:, y, rows_a], dev(dy=-d)) for d in YS]
    w_sib.append(send(wb.at[:, y, rows_a], wb.at[:, y, rows_a], dev(flip=True)))
    across2.wait_recv()
    keys = ingest(2)

    def finish(k):
        total = acc[k, :, 128:256]
        return acc[k, :, 0:128] / total, peak[k] + jnp.log(total) * LOG2E

    part_in = []
    for k in (3, 1, 2):
        unit(k, keys, False)
        mean, lse = finish(k)
        part_s[k - 1] = mean.astype(BF16)
        for t in range(3):
            lse_s[k - 1, :, t * 128 : (t + 1) * 128] = lse[t * 128 : (t + 1) * 128, :].T[0:8, :]
        to = dev(dy=YS[k - 1])
        part_in.append((k, send(part_s.at[k - 1], part_r.at[k - 1], to), send(lse_s.at[k - 1], lse_r.at[k - 1], to)))
    unit(0, keys, False)
    mean0, lse0 = finish(0)
    means, lses = [mean0], [lse0]
    for k, a, b in part_in:
        a.wait_recv()
        b.wait_recv()
        means.append(part_r[k - 1].astype(F32))
        lses.append(
            jnp.concatenate(
                [
                    jnp.broadcast_to(lse_r[k - 1, 0:1, t * 128 : (t + 1) * 128], (128, 128)).T
                    for t in range(3)
                ],
                axis=0,
            )
        )
    best = functools.reduce(jnp.maximum, lses)
    shares = [jnp.exp2(v - best) for v in lses]
    mixed = sum(m * s for m, s in zip(means, shares)) / sum(shares)
    mixed = mixed.astype(BF16)
    for h in range(6):
        heads[:, h * 128 : (h + 1) * 128] = mixed[h * 64 : (h + 1) * 64, :]

    for c, d in zip(w_b2, z_to):
        c.wait_recv()
        at = (z_lo - d + 4) % 4
        w_sib.append(send(wb.at[at, :, rows_b], wb.at[at, :, rows_b], dev(flip=True)))
    for c, d in zip(w_a2, YS):
        c.wait_recv()
        at = (y + d + 4) % 4
        w_sib.append(send(wb.at[:, at, rows_a], wb.at[:, at, rows_a], dev(flip=True)))
    arrived(w_sib)

    def project(to):
        return lax.dot_general(heads[...], wb[to].reshape(768, 768), NT, preferred_element_type=F32)

    sums_in = []
    for k, d in enumerate(XS):
        ps[k] = project((x + d + 4) % 4).astype(BF16)
        sums_in.append(send(ps.at[k], pr.at[k], dev(dx=d)))
    total = project(x)
    for k, c in enumerate(sums_in):
        c.wait_recv()
        total = total + pr[k].astype(F32)
    square = jnp.sum(total * total, axis=1, keepdims=True)
    square = jnp.concatenate([jnp.broadcast_to(square, (64, 128)), jnp.zeros((64, 128), F32)], axis=0)
    pw_s[...] = square.T[0:8, :]
    power_in = [send(pw_s, pw_r.at[k], dev(dx=d)) for k, d in enumerate(XS)]
    level = level_ref[span]
    levels = lax.broadcasted_iota(jnp.int32, gate_ref.shape, 0)
    gate = jnp.sum(jnp.where(levels == level, gate_ref[...], 0.0), axis=0, keepdims=True) * gain_ref[...]
    power = pw_s[...]
    for k, c in enumerate(power_in):
        c.wait_recv()
        power = power + pw_r[k]
    power = jnp.broadcast_to(power[0:1, :], (128, 128)).T[0:64, 0:1] * (1.0 / 3072)
    out_ref[...] = (total * lax.rsqrt(power + 1e-06) * gate).astype(BF16)
    for c in started:
        c.wait_send()


MESSAGES = 64


def local(queries, key_value_pairs, out_weight, gate_table, norm_gain, plan, noise_level, span_mask):
    vmem = pl.BlockSpec(memory_space=pltpu.VMEM)
    smem = pl.BlockSpec(memory_space=pltpu.SMEM)
    return pl.pallas_call(
        kernel,
        out_shape=jax.ShapeDtypeStruct((64, 768), BF16),
        in_specs=[vmem] * 5 + [smem] * 3,
        out_specs=vmem,
        scratch_shapes=[
            pltpu.VMEM((2, 16, 128, 128), BF16),
            pltpu.VMEM((4, 384, 128), BF16),
            pltpu.VMEM((768, 128), BF16),
            pltpu.VMEM((768, 256), BF16),
            pltpu.VMEM((4, 384, 256), F32),
            pltpu.VMEM((4, 384, 128), F32),
            pltpu.VMEM((3, 384, 128), BF16),
            pltpu.VMEM((3, 384, 128), BF16),
            pltpu.VMEM((3, 8, 384), F32),
            pltpu.VMEM((3, 8, 384), F32),
            pltpu.VMEM((64, 768), BF16),
            pltpu.VMEM((4, 4, 192, 768), BF16),
            pltpu.VMEM((3, 64, 768), BF16),
            pltpu.VMEM((3, 64, 768), BF16),
            pltpu.VMEM((8, 128), F32),
            pltpu.VMEM((3, 8, 128), F32),
            pltpu.SemaphoreType.DMA((MESSAGES,)),
            pltpu.SemaphoreType.DMA((MESSAGES,)),
        ],
        compiler_params=pltpu.CompilerParams(
            collective_id=0, has_side_effects=True, vmem_limit_bytes=48 * 2**20
        ),
    )(
        queries,
        key_value_pairs.reshape(128, 128),
        out_weight.T,
        gate_table,
        norm_gain.reshape(1, 768),
        plan,
        noise_level,
        span_mask,
    )


def solution(mesh):
    return jax.shard_map(
        local,
        mesh=mesh,
        in_specs=(
            P(("span", "seq"), "tensor"),
            P(("span", "seq"), None, "tensor"),
            P("tensor", "seq"),
            P(None, "tensor"),
            P("tensor"),
            P(),
            P(),
            P(),
        ),
        out_specs=P(("span", "seq"), "tensor"),
        check_vma=False,
    )
```

time: 551 us -> 76 us (0.14)
  waiting for transfers between devices: 491 us -> 0 us
  Pallas kernels: 0 us -> 70 us
  matrix products: 14.4 us -> 0 us
  between operations: 13.3 us -> 0.02 us
  other arithmetic: 12.7 us -> 0 us
  local copies, waits for them, and re-layouts: 14.3 us -> 5.66 us
    all_gather x2 -> x0, waiting for transfers between devices: 429 us -> none  [the longest x1 368 us: local(): piece = lax.all_gather(key_value_pairs, ('span', 'seq'), axis=0, tiled=True)]
    pallas_call x0 -> x1, Pallas kernels: none -> 70 us  [local(): pl.pallas_call(kernel, out_shape=jax.ShapeDtypeStruct((64, 768), BF16), i...]
    psum x1 -> x0, waiting for transfers between devices: 61.5 us -> none  [local(): lax.psum(partial_sums.astype(jnp.bfloat16), 'tensor').astype(jnp.float32)]
    dot_general x9 -> x0, matrix products: 14.4 us -> none  [the longest x4 7.06 us: update(): jnp.einsum('tkgr,rkd->tkgd', weights.astype(jnp.bfloat16), value_rows, pr...]
    reduce_sum x13 -> x0, other arithmetic: 8.59 us -> none  [the longest x4 2.55 us: update(): total = total * fade + jnp.sum(weights, axis=-1)]
  transfers between devices with their start and end apart: 3 -> 0, of which waited for: 3 -> 0; matrix products, arithmetic and copies ran while one was open for 5% -> 0% of each run, Pallas kernels for 0% -> 0%
where the time goes in v1:
time: 76 us; the launch traced here: 75.6 us
  Pallas kernels  70 us (92%)
  local copies, waits for them, and re-layouts  5.66 us (7%)
    pallas_call x1, Pallas kernels, local(): pl.pallas_call(kernel, out_shape=jax.ShapeDtypeStruct((64, 768), BF16), i...  70 us
    unnamed x15, local copies, waits for them, and re-layouts  4.94 us

profile of v1, /device:TPU:1, one launch (start us, length us, event | category | flops | bytes accessed | tf_op | source)
XLA Modules:
  0.0 75.6 jit_solution(6673061425155944377)
XLA Ops:
  0.0 0.0 copy-start.5
  0.0 0.0 copy-start.6
  0.0 0.7 reshape.7.gain_ref
  0.7 0.0 copy-done.5
  0.7 0.0 copy-done.6
  0.7 0.0 copy-start
  0.7 1.0 %copy-done = bf16[768,192]{0,1:T(8,128)(2,1)S(1)} copy-done((bf16[768,192]{0,1:T(8,128)(2,1)S(1)}, bf16[768,192]{0,1:T(8,128)(2,1)}, u32[]{:S(2)}) %copy-start) | copy-done | bytes 294936
  1.7 0.0 copy-start.1
  1.7 0.9 %copy-done.1 = f32[64,768]{1,0:T(8,128)S(1)} copy-done((f32[64,768]{1,0:T(8,128)S(1)}, f32[64,768]{1,0:T(8,128)}, u32[]{:S(2)}) %copy-start.1) | copy-done | bytes 196632
  2.6 0.0 copy-start.2
  2.6 0.9 %copy-done.2 = bf16[64,768]{1,0:T(8,128)(2,1)S(1)} copy-done((bf16[64,768]{1,0:T(8,128)(2,1)S(1)}, bf16[64,768]{1,0:T(8,128)(2,1)}, u32[]{:S(2)}) %copy-start.2) | copy-done | bytes 98328
  3.5 0.0 copy-start.3
  3.5 0.8 copy-done.3
  4.3 0.0 copy-start.4
  4.3 0.8 copy-done.4
  5.0 70.0 %shard_map.82 = bf16[64,768]{1,0:T(8,128)(2,1)S(1)} custom-call(bf16[64,768]{1,0:T(8,128)(2,1)S(1)} %copy-done.2, bf16[128,128]{1,0:T(8,128)(2,1)S(1)} %bitcast.3, bf16[192,768]{1,0:T(8,128)(2,1)S(1)} %bitcast.2, f32[64,768]{1,0:T(8,128)S(1)} %copy-done.1, f32[1,768]{1,0:T(1,128)S(1)} %reshape.7.gain_ref, s32[8]{0:T(128)S(1)} %copy-done.5, s32[8]{0:T(128)S(1)} %copy-done.6, ...), custom_call_target="tpu_custom_call" | custom-call | tf_op jit(solution)/shard_map/pallas_call | solution.py:239
  75.0 0.6 copy.10
Async XLA Ops:
  0.0 0.7 copy-start.5
  0.0 0.7 copy-start.6
  0.7 1.0 %copy-start = (bf16[768,192]{0,1:T(8,128)(2,1)S(1)}, bf16[768,192]{0,1:T(8,128)(2,1)}, u32[]{:S(2)}) copy-start(bf16[768,192]{0,1:T(8,128)(2,1)} %param.10) | copy-start | bytes 884740
  1.7 0.9 %copy-start.1 = (f32[64,768]{1,0:T(8,128)S(1)}, f32[64,768]{1,0:T(8,128)}, u32[]{:S(2)}) copy-start(f32[64,768]{1,0:T(8,128)} %gate_ref.1) | copy-start | bytes 589828
  2.6 0.9 %copy-start.2 = (bf16[64,768]{1,0:T(8,128)(2,1)S(1)}, bf16[64,768]{1,0:T(8,128)(2,1)}, u32[]{:S(2)}) copy-start(bf16[64,768]{1,0:T(8,128)(2,1)} %q_ref.1) | copy-start | bytes 294916
  3.5 0.8 %copy-start.3 = (bf16[64,2,128]{2,1,0:T(2,128)(2,1)S(1)}, bf16[64,2,128]{2,1,0:T(2,128)(2,1)}, u32[]{:S(2)}) copy-start(bf16[64,2,128]{2,1,0:T(2,128)(2,1)} %param.9) | copy-start | bytes 98308
  4.3 0.8 %copy-start.4 = (s32[8,8,16]{2,1,0:T(8,128)S(1)}, s32[8,8,16]{2,1,0:T(8,128)}, u32[]{:S(2)}) copy-start(s32[8,8,16]{2,1,0:T(8,128)} %mask_ref.1) | copy-start | bytes 12292

commit v2 on v1

--- a/solution.py
+++ b/solution.py
@@ -22,8 +22,8 @@
 
 
 def kernel(
-    q_ref, kv_ref, w_ref, gate_ref, gain_ref, plan_ref, level_ref, mask_ref, out_ref,
-    kvb, qs, kc, vc, acc, peak, part_s, part_r, lse_s, lse_r, heads, wb, ps, pr, pw_s, pw_r,
+    q_hbm, kv_hbm, w_hbm, gate_hbm, gain_hbm, plan_hbm, level_hbm, mask_hbm, out_ref,
+    q_ref, kv_ref, gate_ref, gain_ref, plan_ref, level_ref, mask_ref, ls, kvb, qs, kc, vc, acc, peak, part_s, part_r, lse_s, lse_r, heads, wb, ps, pr, pw_s, pw_r,
     ss, rs,
 ):
     span, seq, x = lax.axis_index("span"), lax.axis_index("seq"), lax.axis_index("tensor")
@@ -42,16 +42,35 @@
     for p in partners:
         pl.semaphore_signal(barrier, inc=1, device_id=p, device_id_type=MESH)
 
+    half = pl.multiple_of(core * 96, 16)
+    rows_a, rows_b = pl.ds(0, 48), pl.ds(48, 48)
+    loads = [
+        pltpu.make_async_copy(src, dst, ls.at[i])
+        for i, (src, dst) in enumerate(
+            [
+                (kv_hbm, kv_ref),
+                (q_hbm, q_ref),
+                (w_hbm.at[pl.ds(half, 96)], wb.at[z_lo, y]),
+                (plan_hbm, plan_ref),
+                (mask_hbm, mask_ref),
+                (level_hbm, level_ref),
+                (gate_hbm, gate_ref),
+                (gain_hbm, gain_ref),
+            ]
+        )
+    ]
+    for c in loads:
+        c.start()
+    loads[0].wait()
     row = lax.broadcasted_iota(jnp.int32, (128, 128), 0)
     col = lax.broadcasted_iota(jnp.int32, (128, 128), 1)
     pick = jnp.where(col == 2 * (row % 64) + row // 64, 1.0, 0.0).astype(BF16)
     kvb[0, 0] = jnp.dot(pick, kv_ref[...], preferred_element_type=F32).astype(BF16)
+    loads[1].wait()
     for h in range(6):
         qs[0, h * 64 : (h + 1) * 64, :] = q_ref[:, h * 128 : (h + 1) * 128]
-    half = pl.multiple_of(core * 96, 16)
-    rows_a = pl.ds(half, 48)
-    rows_b = pl.ds(pl.multiple_of(half + 48, 16), 48)
-    wb[z_lo, y, pl.ds(half, 96), :] = w_ref[pl.ds(half, 96), :]
+    for c in loads[2:]:
+        c.wait()
 
     started = []
 
@@ -82,6 +101,8 @@
     far = [send(kvb.at[0, 0], kvb.at[0, GROUPS[1 + i][0]], dev(dz=-d)) for i, d in enumerate(FAR)]
     near0 = near(0)
     q_in = [send(qs.at[0], qs.at[1 + i], dev(dy=-d)) for i, d in enumerate(YS)]
+    z_to = (-1, 1, 4 * core - 2)
+    w_a1 = [send(wb.at[z_lo, y, rows_a], wb.at[z_lo, y, rows_a], dev(dz=d)) for d in z_to]
     w_b1 = [send(wb.at[z_lo, y, rows_b], wb.at[z_lo, y, rows_b], dev(dy=-d)) for d in YS]
     arrived(near0)
     across0 = across(0)
@@ -89,9 +110,8 @@
     near1, near2 = near(1), near(2)
     far_slot = GROUPS[1][0] + 5 * core
     eighth = send(kvb.at[0, far_slot], kvb.at[0, 15], dev(dz=6 * core - 3))
-    far2 = 4 * core - 2
-    z_to = (-1, 1, far2)
-    w_a1 = [send(wb.at[z_lo, y, rows_a], wb.at[z_lo, y, rows_a], dev(dz=d)) for d in z_to]
+    arrived(w_a1)
+    w_a2 = [send(wb.at[:, y, rows_a], wb.at[:, y, rows_a], dev(dy=-d)) for d in YS]
 
     own_place = plan_ref[span]
 
@@ -137,22 +157,17 @@
     for k in (1, 2, 3):
         unit(k, keys, True)
 
+    arrived(w_b1)
+    w_b2 = [send(wb.at[z_lo, :, rows_b], wb.at[z_lo, :, rows_b], dev(dz=d)) for d in z_to]
     arrived(near1)
     across1 = across(1)
-    arrived(w_b1)
-    w_b2 = [send(wb.at[z_lo, :, rows_b], wb.at[z_lo, :, rows_b], dev(dz=d)) for d in z_to]
-    w_sib = [send(wb.at[z_lo, :, rows_b], wb.at[z_lo, :, rows_b], dev(flip=True))]
+    arrived(near2)
+    eighth.wait_recv()
+    across2 = across(2)
     across1.wait_recv()
     keys = ingest(1)
     for k in range(4):
         unit(k, keys, False)
-
-    arrived(near2)
-    eighth.wait_recv()
-    across2 = across(2)
-    arrived(w_a1)
-    w_a2 = [send(wb.at[:, y, rows_a], wb.at[:, y, rows_a], dev(dy=-d)) for d in YS]
-    w_sib.append(send(wb.at[:, y, rows_a], wb.at[:, y, rows_a], dev(flip=True)))
     across2.wait_recv()
     keys = ingest(2)
 
@@ -190,42 +205,52 @@
     mixed = sum(m * s for m, s in zip(means, shares)) / sum(shares)
     mixed = mixed.astype(BF16)
     for h in range(6):
-        heads[:, h * 128 : (h + 1) * 128] = mixed[h * 64 : (h + 1) * 64, :]
-
-    for c, d in zip(w_b2, z_to):
-        c.wait_recv()
-        at = (z_lo - d + 4) % 4
-        w_sib.append(send(wb.at[at, :, rows_b], wb.at[at, :, rows_b], dev(flip=True)))
-    for c, d in zip(w_a2, YS):
-        c.wait_recv()
-        at = (y + d + 4) % 4
-        w_sib.append(send(wb.at[:, at, rows_a], wb.at[:, at, rows_a], dev(flip=True)))
-    arrived(w_sib)
+        heads[0:64, h * 128 : (h + 1) * 128] = mixed[h * 64 : (h + 1) * 64, :]
+    heads_in = send(heads.at[pl.ds(0, 64)], heads.at[pl.ds(64, 64)], dev(flip=True))
+    arrived(w_a2)
+    arrived(w_b2)
+    heads_in.wait_recv()
 
     def project(to):
-        return lax.dot_general(heads[...], wb[to].reshape(768, 768), NT, preferred_element_type=F32)
-
-    sums_in = []
+        return lax.dot_general(heads[...], wb[to].reshape(384, 768), NT, preferred_element_type=F32)
+
+    mine_in, other_in = [], []
     for k, d in enumerate(XS):
         ps[k] = project((x + d + 4) % 4).astype(BF16)
-        sums_in.append(send(ps.at[k], pr.at[k], dev(dx=d)))
-    total = project(x)
-    for k, c in enumerate(sums_in):
+        own, sibling = pl.ds(0, 64), pl.ds(64, 64)
+        mine_in.append(send(ps.at[k, own], pr.at[k, own], dev(dx=d)))
+        other_in.append(send(ps.at[k, sibling], pr.at[k, sibling], dev(dx=d, flip=True)))
+    last = project(x)
+    ps[3, 64:128, :] = last[64:128, :].astype(BF16)
+    other_in.append(send(ps.at[3, sibling], pr.at[3, sibling], dev(flip=True)))
+    mine = last[0:64, :]
+    for k, c in enumerate(mine_in):
         c.wait_recv()
-        total = total + pr[k].astype(F32)
+        mine = mine + pr[k, 0:64, :].astype(F32)
+    other = jnp.zeros((64, 384), F32)
+    for k, c in enumerate(other_in):
+        c.wait_recv()
+        other = other + pr[k, 64:128, :].astype(F32)
+    halves = (jnp.where(core == 0, mine, other), jnp.where(core == 0, other, mine))
+    total = jnp.concatenate(
+        [v[:, t * 96 : (t + 1) * 96] for t in range(4) for v in halves], axis=1
+    )
     square = jnp.sum(total * total, axis=1, keepdims=True)
     square = jnp.concatenate([jnp.broadcast_to(square, (64, 128)), jnp.zeros((64, 128), F32)], axis=0)
     pw_s[...] = square.T[0:8, :]
     power_in = [send(pw_s, pw_r.at[k], dev(dx=d)) for k, d in enumerate(XS)]
     level = level_ref[span]
     levels = lax.broadcasted_iota(jnp.int32, gate_ref.shape, 0)
-    gate = jnp.sum(jnp.where(levels == level, gate_ref[...], 0.0), axis=0, keepdims=True) * gain_ref[...]
+    gate = jnp.sum(jnp.where(levels == level, gate_ref[...], 0.0), axis=0, keepdims=True)
     power = pw_s[...]
     for k, c in enumerate(power_in):
         c.wait_recv()
         power = power + pw_r[k]
     power = jnp.broadcast_to(power[0:1, :], (128, 128)).T[0:64, 0:1] * (1.0 / 3072)
-    out_ref[...] = (total * lax.rsqrt(power + 1e-06) * gate).astype(BF16)
+    total = total * lax.rsqrt(power + 1e-06)
+    for t in range(6):
+        at = slice(t * 128, (t + 1) * 128)
+        out_ref[:, at] = (total[:, at] * (gain_ref[t : t + 1, :] * gate[:, at])).astype(BF16)
     for c in started:
         c.wait_send()
 
@@ -234,14 +259,21 @@
 
 
 def local(queries, key_value_pairs, out_weight, gate_table, norm_gain, plan, noise_level, span_mask):
-    vmem = pl.BlockSpec(memory_space=pltpu.VMEM)
-    smem = pl.BlockSpec(memory_space=pltpu.SMEM)
+    hbm = pl.BlockSpec(memory_space=pltpu.HBM)
     return pl.pallas_call(
         kernel,
         out_shape=jax.ShapeDtypeStruct((64, 768), BF16),
-        in_specs=[vmem] * 5 + [smem] * 3,
-        out_specs=vmem,
+        in_specs=[hbm] * 8,
+        out_specs=pl.BlockSpec(memory_space=pltpu.VMEM),
         scratch_shapes=[
+            pltpu.VMEM((64, 768), BF16),
+            pltpu.VMEM((128, 128), BF16),
+            pltpu.VMEM((64, 768), F32),
+            pltpu.VMEM((6, 128), F32),
+            pltpu.SMEM((8,), jnp.int32),
+            pltpu.SMEM((8,), jnp.int32),
+            pltpu.SMEM((8, 8, 16), jnp.int32),
+            pltpu.SemaphoreType.DMA((8,)),
             pltpu.VMEM((2, 16, 128, 128), BF16),
             pltpu.VMEM((4, 384, 128), BF16),
             pltpu.VMEM((768, 128), BF16),
@@ -252,24 +284,24 @@
             pltpu.VMEM((3, 384, 128), BF16),
             pltpu.VMEM((3, 8, 384), F32),
             pltpu.VMEM((3, 8, 384), F32),
-            pltpu.VMEM((64, 768), BF16),
-            pltpu.VMEM((4, 4, 192, 768), BF16),
-            pltpu.VMEM((3, 64, 768), BF16),
-            pltpu.VMEM((3, 64, 768), BF16),
+            pltpu.VMEM((128, 768), BF16),
+            pltpu.VMEM((4, 4, 96, 768), BF16),
+            pltpu.VMEM((4, 128, 384), BF16),
+            pltpu.VMEM((4, 128, 384), BF16),
             pltpu.VMEM((8, 128), F32),
             pltpu.VMEM((3, 8, 128), F32),
             pltpu.SemaphoreType.DMA((MESSAGES,)),
             pltpu.SemaphoreType.DMA((MESSAGES,)),
         ],
         compiler_params=pltpu.CompilerParams(
-            collective_id=0, has_side_effects=True, vmem_limit_bytes=48 * 2**20
+            collective_id=0, has_side_effects=True, vmem_limit_bytes=60 * 2**20
         ),
     )(
         queries,
         key_value_pairs.reshape(128, 128),
         out_weight.T,
         gate_table,
-        norm_gain.reshape(1, 768),
+        norm_gain.reshape(6, 128),
         plan,
         noise_level,
         span_mask,

time: 76 us -> 62.1 us (0.82)
  Pallas kernels: 70 us -> 60.4 us
  local copies, waits for them, and re-layouts: 5.66 us -> 1.54 us
    pallas_call x1, Pallas kernels: 70 us -> 60.4 us  [local(): pl.pallas_call(kernel, out_shape=jax.ShapeDtypeStruct((64, 768), BF16), i...]
    unnamed x15 -> x1, local copies, waits for them, and re-layouts: 4.94 us -> 1.54 us
where the time goes in v2:
time: 62.1 us; the launch traced here: 62 us
  Pallas kernels  60.4 us (97%)
  local copies, waits for them, and re-layouts  1.54 us (2%)
    pallas_call x1, Pallas kernels, local(): pl.pallas_call(kernel, out_shape=jax.ShapeDtypeStruct((64, 768), BF16), i...  60.4 us
    unnamed x1, local copies, waits for them, and re-layouts  1.54 us

profile of v2, /device:TPU:1, one launch (start us, length us, event | category | flops | bytes accessed | tf_op | source)
XLA Modules:
  0.0 62.0 jit_solution(9026731463363817862)
XLA Ops:
  0.0 60.4 %shard_map.82 = bf16[64,768]{1,0:T(8,128)(2,1)} custom-call(bf16[64,768]{1,0:T(8,128)(2,1)} %q_hbm.1, bf16[128,128]{1,0:T(8,128)(2,1)} %bitcast.4, bf16[192,768]{1,0:T(8,128)(2,1)} %bitcast.3, f32[64,768]{1,0:T(8,128)} %gate_hbm.1, f32[6,128]{1,0:T(8,128)} %bitcast.5, s32[8]{0:T(128)} %plan_hbm.1, s32[8]{0:T(128)} %level_hbm.1, s32[8,8,16]{2,1,0:T(8,128)} %mask_hbm.1), custom_call_target="tpu_custom_call" | custom-call | tf_op jit(solution)/shard_map/pallas_call | solution.py:263
  60.4 1.5 %copy.10 = bf16[64,768]{1,0:T(8,128)(2,1)} copy(bf16[64,768]{1,0:T(8,128)(2,1)} %shard_map.82) | data formatting | bytes 196608

commit v3 on v2

--- a/solution.py
+++ b/solution.py
@@ -12,12 +12,10 @@
 F32, BF16 = jnp.float32, jnp.bfloat16
 LOG2E = 1.4426950408889634
 SCALE = LOG2E / math.sqrt(128)
-NEAR = (1, -1, 2, -2)
-FAR = (5, -5)
 YS = (1, -1, 2)
 XS = (2, 1, -1)
-SLOTS = (0, 1, -1, 2, -2, 5, 6, 4, 7, 3, -5, -4, -6, -3, -7, 8)
-GROUPS = ((0, 5), (5, 10), (10, 16))
+SLOTS = (0, 1, -1, 3, -3, 2, 4, -2, -4, 6, -6, 5, 7, -5, -7, 8)
+GROUPS = ((0, 4), (4, 10), (10, 16))
 NT = (((1,), (1,)), ((), ()))
 
 
@@ -37,7 +35,7 @@
         return ((zz // 4) * 2 + cc, (zz % 4) * 4 + (y + dy + 4) % 4, (x + dx + 4) % 4)
 
     barrier = pltpu.get_barrier_semaphore()
-    partners = [dev(dz=d) for d in (1, -1, 2, -2, 3, -3, 5, -5)]
+    partners = [dev(dz=d) for d in (1, -1, 2, -2, 3, -3)]
     partners += [dev(dy=d) for d in YS] + [dev(dx=d) for d in XS] + [dev(flip=True)]
     for p in partners:
         pl.semaphore_signal(barrier, inc=1, device_id=p, device_id_type=MESH)
@@ -50,7 +48,7 @@
             [
                 (kv_hbm, kv_ref),
                 (q_hbm, q_ref),
-                (w_hbm.at[pl.ds(half, 96)], wb.at[z_lo, y]),
+                (w_hbm.at[pl.ds(half, 96)], wb.at[0, 0]),
                 (plan_hbm, plan_ref),
                 (mask_hbm, mask_ref),
                 (level_hbm, level_ref),
@@ -83,9 +81,9 @@
         started.append(c)
         return c
 
-    def near(group):
-        lo = GROUPS[group][0]
-        return [send(kvb.at[0, lo], kvb.at[0, lo + 1 + i], dev(dz=-d)) for i, d in enumerate(NEAR)]
+    def pass_on(block, steps):
+        src = kvb.at[0, SLOTS.index(block)]
+        return [send(src, kvb.at[0, SLOTS.index(block - d)], dev(dz=d)) for d in steps]
 
     def across(group):
         lo, hi = GROUPS[group]
@@ -98,20 +96,28 @@
 
     pl.semaphore_wait(barrier, len(partners))
 
-    far = [send(kvb.at[0, 0], kvb.at[0, GROUPS[1 + i][0]], dev(dz=-d)) for i, d in enumerate(FAR)]
-    near0 = near(0)
+    z_to = (-1, 1, 4 * core - 2)
+    far = pass_on(0, (-3, 3))
+    w_a1 = [send(wb.at[0, 0, rows_a], wb.at[1 + i, 0, rows_a], dev(dz=d)) for i, d in enumerate(z_to)]
+    near0 = pass_on(0, (-1, 1))
+    w_b1 = [send(wb.at[0, 0, rows_b], wb.at[0, 1 + i, rows_b], dev(dy=-d)) for i, d in enumerate(YS)]
     q_in = [send(qs.at[0], qs.at[1 + i], dev(dy=-d)) for i, d in enumerate(YS)]
-    z_to = (-1, 1, 4 * core - 2)
-    w_a1 = [send(wb.at[z_lo, y, rows_a], wb.at[z_lo, y, rows_a], dev(dz=d)) for d in z_to]
-    w_b1 = [send(wb.at[z_lo, y, rows_b], wb.at[z_lo, y, rows_b], dev(dy=-d)) for d in YS]
+    w_a2 = [send(wb.at[0, 0, rows_a], wb.at[0, 1 + i, rows_a], dev(dy=-d)) for i, d in enumerate(YS)]
+    arrived(far)
+    relay = pass_on(3, (-3,)) + pass_on(-3, (3,))
+    near1 = pass_on(3, (-1, 1)) + pass_on(-3, (1, -1))
     arrived(near0)
     across0 = across(0)
-    arrived(far)
-    near1, near2 = near(1), near(2)
-    far_slot = GROUPS[1][0] + 5 * core
-    eighth = send(kvb.at[0, far_slot], kvb.at[0, 15], dev(dz=6 * core - 3))
     arrived(w_a1)
-    w_a2 = [send(wb.at[:, y, rows_a], wb.at[:, y, rows_a], dev(dy=-d)) for d in YS]
+    got = pl.ds(1, 3)
+    w_a2 += [send(wb.at[got, 0, rows_a], wb.at[got, 1 + i, rows_a], dev(dy=-d)) for i, d in enumerate(YS)]
+    arrived(relay)
+    near2 = pass_on(6, (-1, 1)) + pass_on(-6, (1, -1))
+    near2.append(send(kvb.at[0, SLOTS.index(6) + core], kvb.at[0, SLOTS.index(8)], dev(dz=4 * core - 2)))
+    arrived(w_b1)
+    w_b2 = [send(wb.at[0, :, rows_b], wb.at[1 + i, :, rows_b], dev(dz=d)) for i, d in enumerate(z_to)]
+    arrived(near1)
+    across1 = across(1)
 
     own_place = plan_ref[span]
 
@@ -132,23 +138,21 @@
         return i * 64
 
     def unit(k, keys, first):
-        for r in range(0, 384, 128):
-            rr = slice(r, r + 128)
-            s = lax.dot_general(qs[k, rr, :], kc[0:keys, :], NT, preferred_element_type=F32)
-            cols = [s[:, t : t + 128] for t in range(0, keys, 128)]
-            top = functools.reduce(jnp.maximum, cols)
-            top = jnp.broadcast_to(jnp.max(top, axis=1, keepdims=True) * SCALE, (128, 128))
-            if not first:
-                old = peak[k, rr, :]
-                top = jnp.maximum(old, top)
-            weights = jnp.concatenate([jnp.exp2(t * SCALE - top).astype(BF16) for t in cols], axis=1)
-            added = jnp.dot(weights, vc[0:keys, :], preferred_element_type=F32)
-            if first:
-                acc[k, rr, :] = added
-            else:
-                fade = jnp.exp2(old - top)
-                acc[k, rr, :] = acc[k, rr, :] * jnp.concatenate([fade, fade], axis=1) + added
-            peak[k, rr, :] = top
+        s = lax.dot_general(qs[k], kc[0:keys, :], NT, preferred_element_type=F32)
+        cols = [s[:, t : t + 128] for t in range(0, keys, 128)]
+        top = functools.reduce(jnp.maximum, cols)
+        top = jnp.broadcast_to(jnp.max(top, axis=1, keepdims=True) * SCALE, (384, 128))
+        if not first:
+            old = peak[k]
+            top = jnp.maximum(old, top)
+        weights = jnp.concatenate([jnp.exp2(t * SCALE - top).astype(BF16) for t in cols], axis=1)
+        added = jnp.dot(weights, vc[0:keys, :], preferred_element_type=F32)
+        if first:
+            acc[k] = added
+        else:
+            fade = jnp.exp2(old - top)
+            acc[k] = acc[k] * jnp.concatenate([fade, fade], axis=1) + added
+        peak[k] = top
 
     across0.wait_recv()
     keys = ingest(0)
@@ -157,12 +161,7 @@
     for k in (1, 2, 3):
         unit(k, keys, True)
 
-    arrived(w_b1)
-    w_b2 = [send(wb.at[z_lo, :, rows_b], wb.at[z_lo, :, rows_b], dev(dz=d)) for d in z_to]
-    arrived(near1)
-    across1 = across(1)
     arrived(near2)
-    eighth.wait_recv()
     across2 = across(2)
     across1.wait_recv()
     keys = ingest(1)
@@ -211,8 +210,13 @@
     arrived(w_b2)
     heads_in.wait_recv()
 
+    def slot_of(to, here):
+        d = (to - here + 4) % 4
+        return jnp.where(d < 2, d, 5 - d)
+
     def project(to):
-        return lax.dot_general(heads[...], wb[to].reshape(384, 768), NT, preferred_element_type=F32)
+        w = jnp.concatenate([wb[slot_of(to, z_lo), slot_of(t, y)] for t in range(4)], axis=0)
+        return lax.dot_general(heads[...], w, NT, preferred_element_type=F32)
 
     mine_in, other_in = [], []
     for k, d in enumerate(XS):

time: 62.1 us -> 56.8 us (0.915)
  Pallas kernels: 60.4 us -> 55 us
    pallas_call x1, Pallas kernels: 60.4 us -> 55 us  [local(): pl.pallas_call(kernel, out_shape=jax.ShapeDtypeStruct((64, 768), BF16), i...]
where the time goes in v3:
time: 56.8 us; the launch traced here: 56.6 us
  Pallas kernels  55 us (97%)
  local copies, waits for them, and re-layouts  1.54 us (3%)
    pallas_call x1, Pallas kernels, local(): pl.pallas_call(kernel, out_shape=jax.ShapeDtypeStruct((64, 768), BF16), i...  55 us
    unnamed x1, local copies, waits for them, and re-layouts  1.54 us

profile of v3, /device:TPU:1, one launch (start us, length us, event | category | flops | bytes accessed | tf_op | source)
XLA Modules:
  0.0 56.6 jit_solution(15950087718944884754)
XLA Ops:
  0.0 55.0 %shard_map.82 = bf16[64,768]{1,0:T(8,128)(2,1)} custom-call(bf16[64,768]{1,0:T(8,128)(2,1)} %q_hbm.1, bf16[128,128]{1,0:T(8,128)(2,1)} %bitcast.4, bf16[192,768]{1,0:T(8,128)(2,1)} %bitcast.3, f32[64,768]{1,0:T(8,128)} %gate_hbm.1, f32[6,128]{1,0:T(8,128)} %bitcast.5, s32[8]{0:T(128)} %plan_hbm.1, s32[8]{0:T(128)} %level_hbm.1, s32[8,8,16]{2,1,0:T(8,128)} %mask_hbm.1), custom_call_target="tpu_custom_call" | custom-call | tf_op jit(solution)/shard_map/pallas_call | solution.py:267
  55.0 1.5 %copy.10 = bf16[64,768]{1,0:T(8,128)(2,1)} copy(bf16[64,768]{1,0:T(8,128)(2,1)} %shard_map.82) | data formatting | bytes 196608

commit v4 on v3

--- a/solution.py
+++ b/solution.py
@@ -41,7 +41,7 @@
         pl.semaphore_signal(barrier, inc=1, device_id=p, device_id_type=MESH)
 
     half = pl.multiple_of(core * 96, 16)
-    rows_a, rows_b = pl.ds(0, 48), pl.ds(48, 48)
+    rows_a, rows_b = pl.ds(0, 32), pl.ds(32, 64)
     loads = [
         pltpu.make_async_copy(src, dst, ls.at[i])
         for i, (src, dst) in enumerate(
@@ -100,12 +100,12 @@
     far = pass_on(0, (-3, 3))
     w_a1 = [send(wb.at[0, 0, rows_a], wb.at[1 + i, 0, rows_a], dev(dz=d)) for i, d in enumerate(z_to)]
     near0 = pass_on(0, (-1, 1))
+    q_in = [send(qs.at[0], qs.at[1 + i], dev(dy=-d)) for i, d in enumerate(YS)]
     w_b1 = [send(wb.at[0, 0, rows_b], wb.at[0, 1 + i, rows_b], dev(dy=-d)) for i, d in enumerate(YS)]
-    q_in = [send(qs.at[0], qs.at[1 + i], dev(dy=-d)) for i, d in enumerate(YS)]
-    w_a2 = [send(wb.at[0, 0, rows_a], wb.at[0, 1 + i, rows_a], dev(dy=-d)) for i, d in enumerate(YS)]
     arrived(far)
     relay = pass_on(3, (-3,)) + pass_on(-3, (3,))
     near1 = pass_on(3, (-1, 1)) + pass_on(-3, (1, -1))
+    w_a2 = [send(wb.at[0, 0, rows_a], wb.at[0, 1 + i, rows_a], dev(dy=-d)) for i, d in enumerate(YS)]
     arrived(near0)
     across0 = across(0)
     arrived(w_a1)
@@ -115,7 +115,7 @@
     near2 = pass_on(6, (-1, 1)) + pass_on(-6, (1, -1))
     near2.append(send(kvb.at[0, SLOTS.index(6) + core], kvb.at[0, SLOTS.index(8)], dev(dz=4 * core - 2)))
     arrived(w_b1)
-    w_b2 = [send(wb.at[0, :, rows_b], wb.at[1 + i, :, rows_b], dev(dz=d)) for i, d in enumerate(z_to)]
+    w_b2 = [send(wb.at[0, :, rows_b], wb.at[1 + i, :, rows_b], dev(dz=d)) for i, d in enumerate((-1, 1))]
     arrived(near1)
     across1 = across(1)
 
@@ -185,6 +185,12 @@
         part_in.append((k, send(part_s.at[k - 1], part_r.at[k - 1], to), send(lse_s.at[k - 1], lse_r.at[k - 1], to)))
     unit(0, keys, False)
     mean0, lse0 = finish(0)
+    arrived(w_b2)
+    low, high = pl.ds(0, 2), pl.ds(2, 2)
+    w_b3 = [
+        send(wb.at[1, low, rows_b], wb.at[3, low, rows_b], dev(dz=-1)),
+        send(wb.at[2, high, rows_b], wb.at[3, high, rows_b], dev(dz=1)),
+    ]
     means, lses = [mean0], [lse0]
     for k, a, b in part_in:
         a.wait_recv()
@@ -207,7 +213,7 @@
         heads[0:64, h * 128 : (h + 1) * 128] = mixed[h * 64 : (h + 1) * 64, :]
     heads_in = send(heads.at[pl.ds(0, 64)], heads.at[pl.ds(64, 64)], dev(flip=True))
     arrived(w_a2)
-    arrived(w_b2)
+    arrived(w_b3)
     heads_in.wait_recv()
 
     def slot_of(to, here):

time: 56.8 us -> 55.7 us (0.981)
  Pallas kernels: 55 us -> 54 us
    pallas_call x1, Pallas kernels: 55 us -> 54 us  [local(): pl.pallas_call(kernel, out_shape=jax.ShapeDtypeStruct((64, 768), BF16), i...]
where the time goes in v4:
time: 55.7 us; the launch traced here: 55.5 us
  Pallas kernels  54 us (97%)
  local copies, waits for them, and re-layouts  1.54 us (3%)
    pallas_call x1, Pallas kernels, local(): pl.pallas_call(kernel, out_shape=jax.ShapeDtypeStruct((64, 768), BF16), i...  54 us
    unnamed x1, local copies, waits for them, and re-layouts  1.54 us

profile of v4, /device:TPU:1, one launch (start us, length us, event | category | flops | bytes accessed | tf_op | source)
XLA Modules:
  0.0 55.5 jit_solution(8197777398398089895)
XLA Ops:
  0.0 54.0 %shard_map.82 = bf16[64,768]{1,0:T(8,128)(2,1)} custom-call(bf16[64,768]{1,0:T(8,128)(2,1)} %q_hbm.1, bf16[128,128]{1,0:T(8,128)(2,1)} %bitcast.4, bf16[192,768]{1,0:T(8,128)(2,1)} %bitcast.3, f32[64,768]{1,0:T(8,128)} %gate_hbm.1, f32[6,128]{1,0:T(8,128)} %bitcast.5, s32[8]{0:T(128)} %plan_hbm.1, s32[8]{0:T(128)} %level_hbm.1, s32[8,8,16]{2,1,0:T(8,128)} %mask_hbm.1), custom_call_target="tpu_custom_call" | custom-call | tf_op jit(solution)/shard_map/pallas_call | solution.py:273
  54.0 1.5 %copy.10 = bf16[64,768]{1,0:T(8,128)(2,1)} copy(bf16[64,768]{1,0:T(8,128)(2,1)} %shard_map.82) | data formatting | bytes 196608

commit v5 on v4

--- a/solution.py
+++ b/solution.py
@@ -102,17 +102,24 @@
     near0 = pass_on(0, (-1, 1))
     q_in = [send(qs.at[0], qs.at[1 + i], dev(dy=-d)) for i, d in enumerate(YS)]
     w_b1 = [send(wb.at[0, 0, rows_b], wb.at[0, 1 + i, rows_b], dev(dy=-d)) for i, d in enumerate(YS)]
-    arrived(far)
-    relay = pass_on(3, (-3,)) + pass_on(-3, (3,))
-    near1 = pass_on(3, (-1, 1)) + pass_on(-3, (1, -1))
+    relay, near1 = [], []
+    far[1].wait_recv()
+    relay += pass_on(-3, (3,))
+    near1 += pass_on(-3, (1, -1))
+    far[0].wait_recv()
+    relay += pass_on(3, (-3,))
+    near1 += pass_on(3, (-1, 1))
     w_a2 = [send(wb.at[0, 0, rows_a], wb.at[0, 1 + i, rows_a], dev(dy=-d)) for i, d in enumerate(YS)]
     arrived(near0)
     across0 = across(0)
     arrived(w_a1)
     got = pl.ds(1, 3)
     w_a2 += [send(wb.at[got, 0, rows_a], wb.at[got, 1 + i, rows_a], dev(dy=-d)) for i, d in enumerate(YS)]
-    arrived(relay)
-    near2 = pass_on(6, (-1, 1)) + pass_on(-6, (1, -1))
+    near2 = []
+    relay[0].wait_recv()
+    near2 += pass_on(-6, (1, -1))
+    relay[1].wait_recv()
+    near2 += pass_on(6, (-1, 1))
     near2.append(send(kvb.at[0, SLOTS.index(6) + core], kvb.at[0, SLOTS.index(8)], dev(dz=4 * core - 2)))
     arrived(w_b1)
     w_b2 = [send(wb.at[0, :, rows_b], wb.at[1 + i, :, rows_b], dev(dz=d)) for i, d in enumerate((-1, 1))]
@@ -121,11 +128,11 @@
 
     own_place = plan_ref[span]
 
-    def ingest(group):
+    def ingest(group, sides=(0, 1)):
         lo, hi = GROUPS[group]
         own_k = kvb[0, 0, 0:64, :]
         i = 0
-        for rc in (0, 1):
+        for rc in sides:
             for slot in range(lo, hi):
                 zz = (z + SLOTS[slot] + 16) % 16
                 there = (zz // 4) * 2 + (core if rc == 0 else 1 - core)
@@ -167,8 +174,11 @@
     keys = ingest(1)
     for k in range(4):
         unit(k, keys, False)
+    keys = ingest(2, (0,))
+    for k in range(4):
+        unit(k, keys, False)
     across2.wait_recv()
-    keys = ingest(2)
+    keys = ingest(2, (1,))
 
     def finish(k):
         total = acc[k, :, 128:256]

time: 55.7 us -> 55.1 us (0.989)
  Pallas kernels: 54 us -> 53.4 us
where the time goes in v5:
time: 55.1 us; the launch traced here: 55 us
  Pallas kernels  53.4 us (97%)
  local copies, waits for them, and re-layouts  1.54 us (3%)
    pallas_call x1, Pallas kernels, local(): pl.pallas_call(kernel, out_shape=jax.ShapeDtypeStruct((64, 768), BF16), i...  53.4 us
    unnamed x1, local copies, waits for them, and re-layouts  1.54 us

profile of v5, /device:TPU:1, one launch (start us, length us, event | category | flops | bytes accessed | tf_op | source)
XLA Modules:
  0.0 55.0 jit_solution(9083276286227370034)
XLA Ops:
  0.0 53.4 %shard_map.82 = bf16[64,768]{1,0:T(8,128)(2,1)} custom-call(bf16[64,768]{1,0:T(8,128)(2,1)} %q_hbm.1, bf16[128,128]{1,0:T(8,128)(2,1)} %bitcast.4, bf16[192,768]{1,0:T(8,128)(2,1)} %bitcast.3, f32[64,768]{1,0:T(8,128)} %gate_hbm.1, f32[6,128]{1,0:T(8,128)} %bitcast.5, s32[8]{0:T(128)} %plan_hbm.1, s32[8]{0:T(128)} %level_hbm.1, s32[8,8,16]{2,1,0:T(8,128)} %mask_hbm.1), custom_call_target="tpu_custom_call" | custom-call | tf_op jit(solution)/shard_map/pallas_call | solution.py:283
  53.4 1.5 %copy.10 = bf16[64,768]{1,0:T(8,128)(2,1)} copy(bf16[64,768]{1,0:T(8,128)(2,1)} %shard_map.82) | data formatting | bytes 196608
